TPU v7x, 128 devices: a whole 4x4x4 slice. The times are simulated.
128 devices in a mesh: tm: 32 (over z, x, y_hi), rows: 4 (over y_lo, core).
Axes of the slice: x: 4, y: 4 (y_hi: 2, y_lo: 2; y = y_hi * 2 + y_lo), z: 4, core: 2. Of those that a mesh axis runs over, the one named last changes fastest.
Arguments:
- video: bfloat16 [256, 32, 128, 128], P('tm', 'rows'), may hold values from -36 to 50
- conv_weight: bfloat16 [3, 3, 3, 128, 256], replicated, may hold values from -0.109375 to 0.109375
- norm_gain: float32 [256], replicated, may hold values from 0.5 to 1.5
- norm_bias: float32 [256], replicated, may hold values from -3 to 3
Outputs:
- patch_tokens: bfloat16 [16, 64, 256, 1024], P('rows', 'tm')
All inputs are finite; a program needn't handle non-finite values.
Results may differ from a plain program's by a relative error of at most 0.0049.
Values may be sent and summed in bfloat16 or wider, within the bound.
A program may use at most 128 MiB of HBM per device.

v0:
```python
import jax
import jax.numpy as jnp
from jax import lax
from jax.sharding import PartitionSpec as P

GROUPS = 32
inv_root = 0.7071067811865476


def from_partner(block, axis, distance):
    count = lax.axis_size(axis)
    route = []
    for low in range(count):
        high = low | 1 << distance
        if high != low and high < count:
            route += [(low, high), (high, low)]
    return lax.ppermute(block, axis, route)


def shifted(block, axis, distance):
    devices = range(lax.axis_size(axis))
    route = [(i - distance, i) for i in devices if i - distance in devices]
    return lax.ppermute(block, axis, route)


def padded_2(cells, sides, width):
    for axis, dim in sides:
        count = lax.axis_size(axis)
        ends = count - 1
        head = lax.slice_in_dim(cells, 0, width, axis=dim)
        tail = lax.slice_in_dim(cells, cells.shape[dim] - width, cells.shape[dim], axis=dim)
        cells = jnp.concatenate(
            [
                lax.ppermute(tail, axis, [(i, (i + 1) % count) for i in range(ends)]),
                cells,
                lax.ppermute(head, axis, [((i + 1) % count, i) for i in range(ends)]),
            ],
            axis=dim,
        )
    return cells


def per_device(video, conv_weight, norm_gain, norm_bias):
    frames, height, width, channels = video.shape
    tm_count = lax.axis_size("tm")
    current = video.astype(jnp.float32)
    position = lax.axis_index("tm")
    for bit_number in range(3):
        partner = from_partner(current, "tm", bit_number)
        is_upper = position >> bit_number & 1 == 1
        current = jnp.where(
            is_upper, (partner - current) * inv_root, (current + partner) * inv_root
        )
    wavelet = current.astype(jnp.bfloat16)
    last_frames = wavelet[frames - 2 :]
    earlier = shifted(last_frames, "tm", 1)
    extended = jnp.concatenate([earlier, wavelet], axis=0)
    with_rows = padded_2(extended, (("rows", 1),), 1)
    padded = jnp.pad(with_rows, ((0, 0), (0, 0), (1, 1), (0, 0)))
    convolved = lax.conv_general_dilated(
        padded[None],
        conv_weight,
        (1, 1, 1),
        "VALID",
        dimension_numbers=("NDHWC", "DHWIO", "NDHWC"),
        preferred_element_type=jnp.float32,
    )[0]
    out_frames, out_height, out_width, out_channels = convolved.shape
    group_count = GROUPS
    groups = convolved.reshape(
        out_frames, out_height, out_width, group_count, out_channels // group_count
    )
    entries = float(
        out_frames
        * out_height
        * out_width
        * (out_channels // group_count)
        * tm_count
        * lax.axis_size("rows")
    )
    local_sums = jnp.sum(groups, axis=(0, 1, 2, 4))
    group_total = lax.psum(local_sums, ("tm", "rows"))
    group_mean = group_total / entries
    centered = groups - group_mean[:, None]
    squares = lax.psum(jnp.sum(centered * centered, axis=(0, 1, 2, 4)), ("tm", "rows"))
    variance = squares / entries
    normed = (centered / jnp.sqrt(variance + 1e-05)[:, None]).reshape(
        out_frames, out_height, out_width, out_channels
    )
    activated = jax.nn.silu(normed * norm_gain + norm_bias).astype(jnp.bfloat16)
    arranged = activated.reshape(
        out_frames, out_height // 2, 2, out_width // 2, 2, out_channels
    ).transpose(1, 3, 0, 2, 4, 5)
    arranged = arranged.reshape(out_height // 2, out_width // 2, out_frames, 4 * out_channels)
    return lax.all_to_all(arranged, "tm", split_axis=1, concat_axis=2, tiled=True)


def solution(mesh):
    placed = (P("tm", "rows", None, None), P(), P(), P())
    return jax.shard_map(
        per_device,
        mesh=mesh,
        in_specs=placed,
        out_specs=P("rows", "tm", None, None),
        check_vma=False,
    )
```

profile of v0, /device:TPU:0, one launch (start us, length us, event | category | flops | bytes accessed | tf_op | source)
XLA Modules:
  0.0 597.1 jit_solution(17662172223809165032)
XLA Ops:
  0.0 0.0 copy-start
  0.0 4.3 convert_element_type.12
  4.3 3.3 collective-permute-start
  7.5 90.9 %collective-permute-done = f32[8,8,128,128]{3,2,1,0:T(8,128)} collective-permute-done((f32[8,8,128,128]{3,2,1,0:T(8,128)}, f32[8,8,128,128]{3,2,1,0:T(8,128)}, u32[]{:S(2)}, u32[]{:S(2)}) %collective-permute-start) | collective-permute-done | bytes 4194336 | tf_op jit(solution)/shard_map/ppermute | solution.py:17
  98.4 5.9 multiply_select_fusion.1
  104.3 1.5 collective-permute-start.1
  105.9 90.2 %collective-permute-done.1 = f32[8,8,128,128]{3,2,1,0:T(8,128)} collective-permute-done((f32[8,8,128,128]{3,2,1,0:T(8,128)}, f32[8,8,128,128]{3,2,1,0:T(8,128)}, u32[]{:S(2)}, u32[]{:S(2)}) %collective-permute-start.1) | collective-permute-done | bytes 4194336 | tf_op jit(solution)/shard_map/ppermute | solution.py:17
  196.1 6.9 %multiply_select_fusion = f32[8,8,128,128]{3,2,1,0:T(8,128)} fusion(f32[8,8,128,128]{3,2,1,0:T(8,128)} %multiply_select_fusion.1, f32[8,8,128,128]{3,2,1,0:T(8,128)} %collective-permute-done.1, pred[]{:T(512)S(6)} %eq.10), kind=kLoop, calls=%fused_computation.15 | loop fusion | flops 5242880 | bytes 12582913 | tf_op jit(solution)/shard_map/jit(_where)/select_n | solution.py:51
  203.0 3.0 collective-permute-start.2
  206.1 89.3 %collective-permute-done.2 = f32[8,8,128,128]{3,2,1,0:T(8,128)} collective-permute-done((f32[8,8,128,128]{3,2,1,0:T(8,128)}, f32[8,8,128,128]{3,2,1,0:T(8,128)}, u32[]{:S(2)}, u32[]{:S(2)}) %collective-permute-start.2) | collective-permute-done | bytes 4194336 | tf_op jit(solution)/shard_map/ppermute | solution.py:17
  295.4 4.5 select_convert_fusion
  299.9 5.1 collective-permute-start.3
  305.1 8.4 %collective-permute-done.3 = bf16[2,8,128,128]{3,2,1,0:T(8,128)(2,1)S(1)} collective-permute-done((bf16[2,8,128,128]{3,2,1,0:T(8,128)(2,1)S(1)}, bf16[2,8,128,128]{3,2,1,0:T(8,128)(2,1)S(1)}, u32[]{:S(2)}, u32[]{:S(2)}) %collective-permute-start.3) | collective-permute-done | bytes 524320 | tf_op jit(solution)/shard_map/ppermute | solution.py:23
  313.5 0.1 pad_maximum_fusion.1
  313.5 1.3 collective-permute-start.4
  314.9 1.3 collective-permute-start.5
  316.2 0.0 collective-permute-done.4
  316.2 3.1 collective-permute-done.5
  319.3 2.1 fusion.13
  321.4 2.0 pad.5
  323.4 6.9 %reshape.19 = bf16[10,10,1,8,17,128]{5,4,3,1,0,2:T(8,128)(2,1)} reshape(bf16[10,10,1,136,128]{4,3,1,0,2:T(8,128)(2,1)} %pad.5) | data formatting | bytes 6963200 | tf_op jit(solution)/shard_map/conv_general_dilated | solution.py:60
  330.4 0.0 copy-start.3
  330.4 3.0 copy.29
  333.4 0.1 slice.15
  333.5 0.0 copy-done
  333.5 0.0 copy-done.3
  333.5 19.0 %select_reduce_fusion.1 = (f32[256]{0:T(256)S(1)}, f32[8,8,8,17,256]{4,2,3,1,0:T(8,128)}) fusion(pred[8,17]{0,1:T(8,128)(4,1)S(1)} %copy-done.3, bf16[3,3,3,128,256]{4,3,2,1,0:T(8,128)(2,1)S(1)} %copy-done, bf16[10,10,1,7,2,128]{5,3,4,1,0,2:T(8,128)(2,1)S(1)} %slice.15, bf16[10,10,1,8,17,128]{5,3,4,1,0,2:T(8,128)(2,1)S(1)} %copy.29), kind=kOutput, calls=%fused_computation.3 | convolution fusion | flops 15419842560 | bytes 14523528 | tf_op jit(solution)/shard_map/conv_general_dilated | solution.py:60
  352.6 0.1 reduce_sum.24
  352.7 0.1 reduce_sum.25
  352.8 75.9 %psum.14 = f32[32]{0:T(128)S(1)} all-reduce(f32[32]{0:T(128)S(1)} %reduce_sum.25), channel_id=1, replica_groups=mesh['tm'=32,'rows'=4] {'tm','rows'}, use_global_device_ids=true, to_apply=%region_2.3 | all-reduce | flops 32 | bytes 256 | tf_op jit(solution)/shard_map/psum | solution.py:82
  428.7 0.1 sub.31
  428.8 0.1 sub.32
  428.8 0.0 copy-start.2
  428.9 6.3 %copy.30 = f32[8,8,8,17,256]{4,1,3,2,0:T(8,128)S(1)} copy(f32[8,8,8,17,256]{4,2,3,1,0:T(8,128)} %get-tuple-element.8) | data formatting | bytes 17825792 | tf_op jit(solution)/shard_map/conv_general_dilated | solution.py:60
  435.2 0.0 copy-done.2
  435.2 1.5 select_reduce_fusion
  436.8 4.1 slice.16
  440.8 0.1 reduce_sum.36
  440.9 0.1 reduce_sum.37
  441.0 0.0 copy-start.4
  441.0 0.0 copy-start.5
  441.0 11.5 %copy.31 = f32[8,8,1,128,256]{4,0,3,1,2:T(8,128)} copy(f32[8,8,1,128,256]{4,1,3,0,2:T(8,128)} %slice.16) | data formatting | bytes 16777216 | tf_op jit(solution)/shard_map/conv_general_dilated | solution.py:60
  452.5 62.4 %psum.15 = f32[32]{0:T(128)S(1)} all-reduce(f32[32]{0:T(128)S(1)} %reduce_sum.37), channel_id=1, replica_groups=mesh['tm'=32,'rows'=4] {'tm','rows'}, use_global_device_ids=true, to_apply=%region_5.6 | all-reduce | flops 32 | bytes 256 | tf_op jit(solution)/shard_map/psum | solution.py:85
  515.0 0.1 div.27
  515.0 0.1 div.28
  515.1 0.0 copy-done.4
  515.2 0.0 copy-done.5
  515.2 6.9 %fusion.5 = bf16[4,64,8,2,2,256]{5,1,4,3,0,2:T(8,128)(2,1)S(1)} fusion(f32[256]{0:T(256)S(1)} %copy-done.4, f32[256]{0:T(256)S(1)} %copy-done.5, f32[256]{0:T(256)S(1)} %div.28, f32[256]{0:T(256)S(1)} %sub.32, f32[8,4,2,64,2,256]{5,0,4,3,2,1:T(8,128)} %bitcast.27), kind=kLoop, calls=%fused_computation.17 | loop fusion | flops 18874368 | bytes 12587008 | tf_op jit(solution)/shard_map/transpose | solution.py:93
  522.0 6.4 %copy.37 = bf16[4,64,8,2,2,256]{5,4,3,2,0,1:T(2,128)(2,1)} copy(bf16[4,64,8,2,2,256]{5,1,4,3,0,2:T(8,128)(2,1)S(1)} %fusion.5) | data formatting | bytes 8388608 | tf_op jit(solution)/shard_map/reshape | solution.py:94
  528.4 7.7 %reshape.33 = bf16[4,64,8,1024]{3,2,0,1:T(8,128)(2,1)} reshape(bf16[4,64,8,2,2,256]{5,4,3,2,0,1:T(2,128)(2,1)} %copy.37) | data formatting | bytes 8388608 | tf_op jit(solution)/shard_map/reshape | solution.py:94
  536.1 58.5 %all_to_all.18 = bf16[4,64,8,1024]{3,2,0,1:T(8,128)(2,1)S(1)} all-to-all(bf16[4,64,8,1024]{3,2,0,1:T(8,128)(2,1)} %reshape.33), channel_id=1, replica_groups=mesh['tm'=32,'rows'=4] {'tm'}, dimensions={1} | all-to-all | bytes 8388608 | tf_op jit(solution)/shard_map/all_to_all | solution.py:95
  594.6 0.0 copy-start.1
  594.6 2.5 copy.52
  597.1 0.0 copy-done.1
  (3 shorter events, 0.0 us)
Async XLA Ops:
  0.0 333.5 %copy-start = (bf16[3,3,3,128,256]{4,3,2,1,0:T(8,128)(2,1)S(1)}, bf16[3,3,3,128,256]{4,3,2,1,0:T(8,128)(2,1)}, u32[]{:S(2)}) copy-start(bf16[3,3,3,128,256]{4,3,2,1,0:T(8,128)(2,1)} %param.5) | copy-start | bytes 5308420
  4.3 94.2 %collective-permute-start = (f32[8,8,128,128]{3,2,1,0:T(8,128)}, f32[8,8,128,128]{3,2,1,0:T(8,128)}, u32[]{:S(2)}, u32[]{:S(2)}) collective-permute-start(f32[8,8,128,128]{3,2,1,0:T(8,128)} %convert_element_type.12), channel_id=1, source_target_pairs={{0,4},{4,0},{8,12},{12,8},{16,20},{20,16},{24,28},{28,24},{32,36},... | collective-permute-start | bytes 12582920 | tf_op jit(solution)/shard_map/ppermute | solution.py:17
  104.3 91.8 %collective-permute-start.1 = (f32[8,8,128,128]{3,2,1,0:T(8,128)}, f32[8,8,128,128]{3,2,1,0:T(8,128)}, u32[]{:S(2)}, u32[]{:S(2)}) collective-permute-start(f32[8,8,128,128]{3,2,1,0:T(8,128)} %multiply_select_fusion.1), channel_id=1, source_target_pairs={{0,8},{8,0},{4,12},{12,4},{16,24},{24,16},{20,28},{28,20},{32,40},... | collective-permute-start | bytes 12582920 | tf_op jit(solution)/shard_map/ppermute | solution.py:17
  203.0 92.4 %collective-permute-start.2 = (f32[8,8,128,128]{3,2,1,0:T(8,128)}, f32[8,8,128,128]{3,2,1,0:T(8,128)}, u32[]{:S(2)}, u32[]{:S(2)}) collective-permute-start(f32[8,8,128,128]{3,2,1,0:T(8,128)} %multiply_select_fusion), channel_id=1, source_target_pairs={{0,16},{16,0},{4,20},{20,4},{8,24},{24,8},{12,28},{28,12},{32,48},... | collective-permute-start | bytes 12582920 | tf_op jit(solution)/shard_map/ppermute | solution.py:17
  299.9 13.5 %collective-permute-start.3 = (bf16[2,8,128,128]{3,2,1,0:T(8,128)(2,1)S(1)}, bf16[2,8,128,128]{3,2,1,0:T(8,128)(2,1)S(1)}, u32[]{:S(2)}, u32[]{:S(2)}) collective-permute-start(bf16[2,8,128,128]{3,2,1,0:T(8,128)(2,1)S(1)} %slice.14), channel_id=1, source_target_pairs={{0,4},{4,8},{8,12},{12,16},{16,20},{20,24},{24,28},{28,32},{32,36}... | collective-permute-start | bytes 1572872 | tf_op jit(solution)/shard_map/ppermute | solution.py:23
  313.5 2.6 collective-permute-start.4
  314.9 4.4 collective-permute-start.5
  330.4 3.2 copy-start.3
  428.8 6.4 %copy-start.2 = (f32[8,8,8,17,256]{4,2,3,1,0:T(8,128)S(1)}, f32[8,8,8,17,256]{4,2,3,1,0:T(8,128)}, u32[]{:S(2)}) copy-start(f32[8,8,8,17,256]{4,2,3,1,0:T(8,128)} %get-tuple-element.8) | copy-start | bytes 26738692
  441.0 74.1 %copy-start.4 = (f32[256]{0:T(256)S(1)}, f32[256]{0:T(256)}, u32[]{:S(2)}) copy-start(f32[256]{0:T(256)} %param.7) | copy-start | bytes 3076
  441.0 74.1 %copy-start.5 = (f32[256]{0:T(256)S(1)}, f32[256]{0:T(256)}, u32[]{:S(2)}) copy-start(f32[256]{0:T(256)} %param.6) | copy-start | bytes 3076
  594.6 2.5 copy-start.1
where the time goes:
time: 598 us; the launch traced here: 597 us
  waiting for transfers between devices  282 us (47%)
  blocking collectives  197 us (33%)
  local copies, waits for them, and re-layouts  51 us (9%)
  other arithmetic  32.4 us (5%)
  matrix products  19 us (3%)
  starting transfers between devices  15.6 us (3%)
    ppermute x3, waiting for transfers between devices, from_partner(): return lax.ppermute(block, axis, route)  270 us
    psum x1, blocking collectives, per_device(): group_total = lax.psum(local_sums, ('tm', 'rows'))  75.9 us
    psum x1, blocking collectives, per_device(): lax.psum(jnp.sum(centered * centered, axis=(0, 1, 2, 4)), ('tm', 'rows'))  62.4 us
    all_to_all x1, blocking collectives, per_device(): lax.all_to_all(arranged, 'tm', split_axis=1, concat_axis=2, tiled=True)  58.5 us
    conv_general_dilated x6, local copies, waits for them, and re-layouts, per_device(): lax.conv_general_dilated(padded[None], conv_weight, (1, 1, 1), 'VALID', d...  31.9 us
    conv_general_dilated x1, matrix products, per_device(): lax.conv_general_dilated(padded[None], conv_weight, (1, 1, 1), 'VALID', d...  19 us
    reshape x2, local copies, waits for them, and re-layouts, per_device(): arranged.reshape(out_height // 2, out_width // 2, out_frames, 4 * out_cha...  14.1 us
    select_n x2, other arithmetic, per_device(): jnp.where(is_upper, (partner - current) * inv_root, (current + partner) *...  12.8 us
  transfers between devices with their start and end apart: 6, of which 5 were waited for; matrix products, arithmetic and copies ran while one was open for 0% of the time, Pallas kernels for 0%

commit v1 on v0

--- a/solution.py
+++ b/solution.py
@@ -79,7 +79,7 @@
         * lax.axis_size("rows")
     )
     local_sums = jnp.sum(groups, axis=(0, 1, 2, 4))
-    group_total = lax.psum(local_sums, ("tm", "rows"))
+    group_total = lax.psum(lax.psum(local_sums, "rows"), "tm")
     group_mean = group_total / entries
     centered = groups - group_mean[:, None]
     squares = lax.psum(jnp.sum(centered * centered, axis=(0, 1, 2, 4)), ("tm", "rows"))

time: 598 us -> 632 us (1.057)
  blocking collectives: 197 us -> 231 us
    psum x1 -> x2, blocking collectives: 75.9 us -> 110 us  [per_device(): group_total = lax.psum(lax.psum(local_sums, 'rows'), 'tm')]
where the time goes in v1:
time: 632 us; the launch traced here: 631 us
  waiting for transfers between devices  282 us (45%)
  blocking collectives  231 us (37%)
  local copies, waits for them, and re-layouts  51.1 us (8%)
  other arithmetic  32.4 us (5%)
  matrix products  19 us (3%)
  starting transfers between devices  15.6 us (2%)
    ppermute x3, waiting for transfers between devices, from_partner(): return lax.ppermute(block, axis, route)  270 us
    psum x2, blocking collectives, per_device(): group_total = lax.psum(lax.psum(local_sums, 'rows'), 'tm')  110 us
    psum x1, blocking collectives, per_device(): lax.psum(jnp.sum(centered * centered, axis=(0, 1, 2, 4)), ('tm', 'rows'))  62.7 us
    all_to_all x1, blocking collectives, per_device(): lax.all_to_all(arranged, 'tm', split_axis=1, concat_axis=2, tiled=True)  58 us
    conv_general_dilated x6, local copies, waits for them, and re-layouts, per_device(): lax.conv_general_dilated(padded[None], conv_weight, (1, 1, 1), 'VALID', d...  31.9 us
    conv_general_dilated x1, matrix products, per_device(): lax.conv_general_dilated(padded[None], conv_weight, (1, 1, 1), 'VALID', d...  19 us
    reshape x2, local copies, waits for them, and re-layouts, per_device(): arranged.reshape(out_height // 2, out_width // 2, out_frames, 4 * out_cha...  14.1 us
    select_n x2, other arithmetic, per_device(): jnp.where(is_upper, (partner - current) * inv_root, (current + partner) *...  12.8 us
  transfers between devices with their start and end apart: 6, of which 5 were waited for; matrix products, arithmetic and copies ran while one was open for 0% of the time, Pallas kernels for 0%

profile of v1, /device:TPU:0, one launch (start us, length us, event | category | flops | bytes accessed | tf_op | source)
XLA Modules:
  0.0 631.1 jit_solution(9237313571272716863)
XLA Ops:
  0.0 0.0 copy-start
  0.0 4.3 convert_element_type.12
  4.3 3.3 collective-permute-start
  7.5 90.9 %collective-permute-done = f32[8,8,128,128]{3,2,1,0:T(8,128)} collective-permute-done((f32[8,8,128,128]{3,2,1,0:T(8,128)}, f32[8,8,128,128]{3,2,1,0:T(8,128)}, u32[]{:S(2)}, u32[]{:S(2)}) %collective-permute-start) | collective-permute-done | bytes 4194336 | tf_op jit(solution)/shard_map/ppermute | solution.py:17
  98.4 5.9 multiply_select_fusion.1
  104.3 1.5 collective-permute-start.1
  105.9 90.2 %collective-permute-done.1 = f32[8,8,128,128]{3,2,1,0:T(8,128)} collective-permute-done((f32[8,8,128,128]{3,2,1,0:T(8,128)}, f32[8,8,128,128]{3,2,1,0:T(8,128)}, u32[]{:S(2)}, u32[]{:S(2)}) %collective-permute-start.1) | collective-permute-done | bytes 4194336 | tf_op jit(solution)/shard_map/ppermute | solution.py:17
  196.1 6.9 %multiply_select_fusion = f32[8,8,128,128]{3,2,1,0:T(8,128)} fusion(f32[8,8,128,128]{3,2,1,0:T(8,128)} %multiply_select_fusion.1, f32[8,8,128,128]{3,2,1,0:T(8,128)} %collective-permute-done.1, pred[]{:T(512)S(6)} %eq.10), kind=kLoop, calls=%fused_computation.15 | loop fusion | flops 5242880 | bytes 12582913 | tf_op jit(solution)/shard_map/jit(_where)/select_n | solution.py:51
  203.0 3.0 collective-permute-start.2
  206.1 89.3 %collective-permute-done.2 = f32[8,8,128,128]{3,2,1,0:T(8,128)} collective-permute-done((f32[8,8,128,128]{3,2,1,0:T(8,128)}, f32[8,8,128,128]{3,2,1,0:T(8,128)}, u32[]{:S(2)}, u32[]{:S(2)}) %collective-permute-start.2) | collective-permute-done | bytes 4194336 | tf_op jit(solution)/shard_map/ppermute | solution.py:17
  295.4 4.5 select_convert_fusion
  299.9 5.1 collective-permute-start.3
  305.1 8.4 %collective-permute-done.3 = bf16[2,8,128,128]{3,2,1,0:T(8,128)(2,1)S(1)} collective-permute-done((bf16[2,8,128,128]{3,2,1,0:T(8,128)(2,1)S(1)}, bf16[2,8,128,128]{3,2,1,0:T(8,128)(2,1)S(1)}, u32[]{:S(2)}, u32[]{:S(2)}) %collective-permute-start.3) | collective-permute-done | bytes 524320 | tf_op jit(solution)/shard_map/ppermute | solution.py:23
  313.5 0.1 pad_maximum_fusion.1
  313.5 1.3 collective-permute-start.4
  314.9 1.3 collective-permute-start.5
  316.2 0.0 collective-permute-done.4
  316.2 3.1 collective-permute-done.5
  319.3 2.1 fusion.13
  321.4 2.0 pad.5
  323.4 6.9 %reshape.19 = bf16[10,10,1,8,17,128]{5,4,3,1,0,2:T(8,128)(2,1)} reshape(bf16[10,10,1,136,128]{4,3,1,0,2:T(8,128)(2,1)} %pad.5) | data formatting | bytes 6963200 | tf_op jit(solution)/shard_map/conv_general_dilated | solution.py:60
  330.4 0.0 copy-start.3
  330.4 3.0 copy.29
  333.4 0.1 slice.15
  333.5 0.0 copy-done
  333.5 0.0 copy-done.3
  333.5 19.0 %select_reduce_fusion.1 = (f32[256]{0:T(256)S(1)}, f32[8,8,8,17,256]{4,2,3,1,0:T(8,128)}) fusion(pred[8,17]{0,1:T(8,128)(4,1)S(1)} %copy-done.3, bf16[3,3,3,128,256]{4,3,2,1,0:T(8,128)(2,1)S(1)} %copy-done, bf16[10,10,1,7,2,128]{5,3,4,1,0,2:T(8,128)(2,1)S(1)} %slice.15, bf16[10,10,1,8,17,128]{5,3,4,1,0,2:T(8,128)(2,1)S(1)} %copy.29), kind=kOutput, calls=%fused_computation.3 | convolution fusion | flops 15419842560 | bytes 14523528 | tf_op jit(solution)/shard_map/conv_general_dilated | solution.py:60
  352.6 0.1 reduce_sum.24
  352.7 0.1 reduce_sum.25
  352.8 11.0 %psum.21 = f32[32]{0:T(128)S(1)} all-reduce(f32[32]{0:T(128)S(1)} %reduce_sum.25), channel_id=1, replica_groups=mesh['tm'=32,'rows'=4] {'rows'}, use_global_device_ids=true, to_apply=%region_2.3 | all-reduce | flops 32 | bytes 256 | tf_op jit(solution)/shard_map/psum | solution.py:82
  363.8 99.3 %psum.22 = f32[32]{0:T(128)S(1)} all-reduce(f32[32]{0:T(128)S(1)} %psum.21), channel_id=1, replica_groups=mesh['tm'=32,'rows'=4] {'tm'}, use_global_device_ids=true, to_apply=%region_3.4 | all-reduce | flops 32 | bytes 256 | tf_op jit(solution)/shard_map/psum | solution.py:82
  463.1 0.1 sub.31
  463.2 0.1 sub.32
  463.3 0.0 copy-start.2
  463.3 6.3 %copy.30 = f32[8,8,8,17,256]{4,1,3,2,0:T(8,128)S(1)} copy(f32[8,8,8,17,256]{4,2,3,1,0:T(8,128)} %get-tuple-element.8) | data formatting | bytes 17825792 | tf_op jit(solution)/shard_map/conv_general_dilated | solution.py:60
  469.6 0.0 copy-done.2
  469.6 1.5 select_reduce_fusion
  471.2 4.1 slice.16
  475.2 0.1 reduce_sum.36
  475.3 0.1 reduce_sum.37
  475.4 0.0 copy-start.4
  475.4 0.0 copy-start.5
  475.4 11.5 %copy.31 = f32[8,8,1,128,256]{4,0,3,1,2:T(8,128)} copy(f32[8,8,1,128,256]{4,1,3,0,2:T(8,128)} %slice.16) | data formatting | bytes 16777216 | tf_op jit(solution)/shard_map/conv_general_dilated | solution.py:60
  486.9 62.7 %psum.23 = f32[32]{0:T(128)S(1)} all-reduce(f32[32]{0:T(128)S(1)} %reduce_sum.37), channel_id=1, replica_groups=mesh['tm'=32,'rows'=4] {'tm','rows'}, use_global_device_ids=true, to_apply=%region_6.7 | all-reduce | flops 32 | bytes 256 | tf_op jit(solution)/shard_map/psum | solution.py:85
  549.6 0.1 div.27
  549.6 0.1 div.28
  549.7 0.0 copy-done.4
  549.8 0.0 copy-done.5
  549.8 6.9 %fusion.5 = bf16[4,64,8,2,2,256]{5,1,4,3,0,2:T(8,128)(2,1)S(1)} fusion(f32[256]{0:T(256)S(1)} %copy-done.4, f32[256]{0:T(256)S(1)} %copy-done.5, f32[256]{0:T(256)S(1)} %div.28, f32[256]{0:T(256)S(1)} %sub.32, f32[8,4,2,64,2,256]{5,0,4,3,2,1:T(8,128)} %bitcast.27), kind=kLoop, calls=%fused_computation.17 | loop fusion | flops 18874368 | bytes 12587008 | tf_op jit(solution)/shard_map/transpose | solution.py:93
  556.6 6.4 %copy.37 = bf16[4,64,8,2,2,256]{5,4,3,2,0,1:T(2,128)(2,1)} copy(bf16[4,64,8,2,2,256]{5,1,4,3,0,2:T(8,128)(2,1)S(1)} %fusion.5) | data formatting | bytes 8388608 | tf_op jit(solution)/shard_map/reshape | solution.py:94
  563.0 7.7 %reshape.33 = bf16[4,64,8,1024]{3,2,0,1:T(8,128)(2,1)} reshape(bf16[4,64,8,2,2,256]{5,4,3,2,0,1:T(2,128)(2,1)} %copy.37) | data formatting | bytes 8388608 | tf_op jit(solution)/shard_map/reshape | solution.py:94
  570.7 58.0 %all_to_all.18 = bf16[4,64,8,1024]{3,2,0,1:T(8,128)(2,1)S(1)} all-to-all(bf16[4,64,8,1024]{3,2,0,1:T(8,128)(2,1)} %reshape.33), channel_id=1, replica_groups=mesh['tm'=32,'rows'=4] {'tm'}, dimensions={1} | all-to-all | bytes 8388608 | tf_op jit(solution)/shard_map/all_to_all | solution.py:95
  628.7 0.0 copy-start.1
  628.7 2.5 copy.52
  631.1 0.0 copy-done.1
  (3 shorter events, 0.1 us)
Async XLA Ops:
  0.0 333.5 %copy-start = (bf16[3,3,3,128,256]{4,3,2,1,0:T(8,128)(2,1)S(1)}, bf16[3,3,3,128,256]{4,3,2,1,0:T(8,128)(2,1)}, u32[]{:S(2)}) copy-start(bf16[3,3,3,128,256]{4,3,2,1,0:T(8,128)(2,1)} %param.5) | copy-start | bytes 5308420
  4.3 94.2 %collective-permute-start = (f32[8,8,128,128]{3,2,1,0:T(8,128)}, f32[8,8,128,128]{3,2,1,0:T(8,128)}, u32[]{:S(2)}, u32[]{:S(2)}) collective-permute-start(f32[8,8,128,128]{3,2,1,0:T(8,128)} %convert_element_type.12), channel_id=1, source_target_pairs={{0,4},{4,0},{8,12},{12,8},{16,20},{20,16},{24,28},{28,24},{32,36},... | collective-permute-start | bytes 12582920 | tf_op jit(solution)/shard_map/ppermute | solution.py:17
  104.3 91.8 %collective-permute-start.1 = (f32[8,8,128,128]{3,2,1,0:T(8,128)}, f32[8,8,128,128]{3,2,1,0:T(8,128)}, u32[]{:S(2)}, u32[]{:S(2)}) collective-permute-start(f32[8,8,128,128]{3,2,1,0:T(8,128)} %multiply_select_fusion.1), channel_id=1, source_target_pairs={{0,8},{8,0},{4,12},{12,4},{16,24},{24,16},{20,28},{28,20},{32,40},... | collective-permute-start | bytes 12582920 | tf_op jit(solution)/shard_map/ppermute | solution.py:17
  203.0 92.4 %collective-permute-start.2 = (f32[8,8,128,128]{3,2,1,0:T(8,128)}, f32[8,8,128,128]{3,2,1,0:T(8,128)}, u32[]{:S(2)}, u32[]{:S(2)}) collective-permute-start(f32[8,8,128,128]{3,2,1,0:T(8,128)} %multiply_select_fusion), channel_id=1, source_target_pairs={{0,16},{16,0},{4,20},{20,4},{8,24},{24,8},{12,28},{28,12},{32,48},... | collective-permute-start | bytes 12582920 | tf_op jit(solution)/shard_map/ppermute | solution.py:17
  299.9 13.5 %collective-permute-start.3 = (bf16[2,8,128,128]{3,2,1,0:T(8,128)(2,1)S(1)}, bf16[2,8,128,128]{3,2,1,0:T(8,128)(2,1)S(1)}, u32[]{:S(2)}, u32[]{:S(2)}) collective-permute-start(bf16[2,8,128,128]{3,2,1,0:T(8,128)(2,1)S(1)} %slice.14), channel_id=1, source_target_pairs={{0,4},{4,8},{8,12},{12,16},{16,20},{20,24},{24,28},{28,32},{32,36}... | collective-permute-start | bytes 1572872 | tf_op jit(solution)/shard_map/ppermute | solution.py:23
  313.5 2.6 collective-permute-start.4
  314.9 4.4 collective-permute-start.5
  330.4 3.2 copy-start.3
  463.3 6.4 %copy-start.2 = (f32[8,8,8,17,256]{4,2,3,1,0:T(8,128)S(1)}, f32[8,8,8,17,256]{4,2,3,1,0:T(8,128)}, u32[]{:S(2)}) copy-start(f32[8,8,8,17,256]{4,2,3,1,0:T(8,128)} %get-tuple-element.8) | copy-start | bytes 26738692
  475.4 74.3 %copy-start.4 = (f32[256]{0:T(256)S(1)}, f32[256]{0:T(256)}, u32[]{:S(2)}) copy-start(f32[256]{0:T(256)} %param.7) | copy-start | bytes 3076
  475.4 74.3 %copy-start.5 = (f32[256]{0:T(256)S(1)}, f32[256]{0:T(256)}, u32[]{:S(2)}) copy-start(f32[256]{0:T(256)} %param.6) | copy-start | bytes 3076
  628.7 2.5 copy-start.1
